TPU v7x, 32 devices: a whole 2x2x4 slice. The times are simulated.
32 devices in a mesh: parts: 2 (over y), ctx: 4 (over z), head: 4 (over x, core).
Axes of the slice: x: 2, y: 2, z: 4, core: 2. Of those that a mesh axis runs over, the one named last changes fastest.
Arguments:
- event_ids: int32 [8192], P(('parts', 'ctx')), parts along dimension 0, may hold values from 0 to 255
- embed_table: bfloat16 [256, 1024], replicated, may hold values from -6 to 6
- w_qkv: bfloat16 [1024, 3072], P(None, 'head'), may hold values from -0.1875 to 0.1875
- norm_gain: float32 [1024], P('head'), may hold values from 0.1 to 1.9
- w_out: bfloat16 [1024, 1024], P('head'), may hold values from -0.1875 to 0.1875
- init_state: float32 [8, 128, 128], P('head'), may hold values from -6 to 6
- out_grad: bfloat16 [8192, 1024], P(('parts', 'ctx')), parts along dimension 0, may hold values from -1 to 1
Outputs:
- layer_out: bfloat16 [8192, 1024], P(('parts', 'ctx'), 'head'), parts along dimension 0
- grad_wqkv: float32 [2048, 3072], P(('parts', 'ctx'), 'head'), parts along dimension 0
- grad_wout: float32 [2048, 1024], P(('parts', 'head'), 'ctx'), parts along dimension 0
- grad_gain: float32 [2048], P(('parts', 'head')), parts along dimension 0
- grad_init: float32 [16, 128, 128], P(('parts', 'head')), parts along dimension 0
- grad_table: float32 [512, 1024], P('parts'), parts along dimension 0
There are 2 independent parts, one for each index of `parts`. A program takes and returns all parts, laid end to end along the dimension named above; an argument that names none is the same for every part. Nothing has to cross between parts.
All inputs are finite; a program needn't handle non-finite values.
Results may differ from a plain program's by a relative error of at most 0.0082.
Values sent between devices are 32-bit elements; how exact they have to be, the bound alone decides.
A program may use at most 64 MiB of HBM per device.

v0:
```python
import jax
import jax.numpy as jnp
from jax import lax
from jax.sharding import PartitionSpec as P

BLOCK = 128


EPS = 1e-05


def prefix(part, axis, combine, identity, reverse):
    count = lax.axis_size(axis)
    place = lax.axis_index(axis)
    ahead = count - 1 - place if reverse else place
    gathered = lax.all_gather(part, axis)
    state = jnp.zeros_like(part) + jnp.asarray(identity, part.dtype)

    def one(step, state):
        source = count - 1 - step if reverse else step
        return combine(state, lax.dynamic_index_in_dim(gathered, source, 0, False))

    return lax.fori_loop(0, ahead, one, state)


def lower_mask(block_len):
    rows_idx = lax.broadcasted_iota(jnp.int32, (block_len, block_len), 0)
    cols_idx = lax.broadcasted_iota(jnp.int32, (block_len, block_len), 1)
    return rows_idx >= cols_idx


def add_states(earlier, later_one):
    return earlier + later_one


def contract_rows(left, right):
    return lax.dot_general(
        left, right, (((0,), (0,)), ((), ())), preferred_element_type=jnp.float32
    )


def contract_cols(left, right):
    return lax.dot_general(
        left, right, (((1,), (1,)), ((), ())), preferred_element_type=jnp.float32
    )


def per_device(event_ids, embed_table, w_qkv, norm_gain, w_out, init_state, out_grad):
    highest = lax.Precision.HIGHEST
    tok_rows = event_ids.shape[0]
    vocab_size = embed_table.shape[0]
    head_local = init_state.shape[0]
    head_dim = init_state.shape[1]
    block_len = BLOCK
    blocks = tok_rows // block_len
    one_hot = event_ids[:, None] == lax.broadcasted_iota(jnp.int32, (1, vocab_size), 1)
    embedded = jnp.dot(
        one_hot.astype(jnp.bfloat16), embed_table, preferred_element_type=jnp.float32
    ).astype(jnp.bfloat16)
    projected = jnp.dot(embedded, w_qkv, preferred_element_type=jnp.float32).astype(jnp.bfloat16)
    shaped = projected.reshape(blocks, block_len, head_local, 3, head_dim)
    queries = shaped[:, :, :, 0]
    key_rows = shaped[:, :, :, 1]
    value_rows = shaped[:, :, :, 2]
    block_kv = jnp.einsum(
        "bshd,bshe->bhde", key_rows, value_rows, preferred_element_type=jnp.float32
    )
    own_total = jnp.sum(block_kv, axis=0)
    zero_state = jnp.zeros_like(own_total)
    earlier_state = prefix(own_total, "ctx", add_states, zero_state, False)
    cumulative = jnp.cumsum(block_kv, axis=0)
    shifted = jnp.concatenate([jnp.zeros_like(block_kv[:1]), cumulative[:-1]], axis=0)
    states = init_state[None] + earlier_state[None] + shifted
    mask_tri = lower_mask(block_len)[None, None]
    scores = jnp.einsum("bthd,bshd->bhts", queries, key_rows, preferred_element_type=jnp.float32)
    scores_bf = jnp.where(mask_tri, scores, 0.0).astype(jnp.bfloat16)
    inter = jnp.einsum("bthd,bhde->bthe", queries.astype(jnp.float32), states, precision=highest)
    intra = jnp.einsum("bhts,bshe->bthe", scores_bf, value_rows, preferred_element_type=jnp.float32)
    raw_out = inter + intra
    inv_rms = lax.rsqrt(jnp.mean(raw_out * raw_out, axis=-1, keepdims=True) + EPS)
    normed = raw_out * inv_rms
    gain_view = norm_gain.reshape(head_local, head_dim)
    attn = (normed * gain_view).astype(jnp.bfloat16).reshape(tok_rows, head_local * head_dim)
    head_terms = jnp.dot(attn, w_out, preferred_element_type=jnp.float32)
    mixed = lax.psum_scatter(head_terms, "head", scatter_dimension=1, tiled=True)
    out_cols = mixed.shape[1]
    residual = lax.dynamic_slice_in_dim(embedded, lax.axis_index("head") * out_cols, out_cols, 1)
    layer_out = (residual.astype(jnp.float32) + mixed).astype(jnp.bfloat16)
    grad_attn = contract_cols(out_grad, w_out)
    grad_wout_local = contract_rows(attn, out_grad)
    normed_flat = normed.reshape(tok_rows, head_local * head_dim)
    grad_gain_local = jnp.sum(grad_attn * normed_flat, axis=0)
    grad_norm = (grad_attn * norm_gain).reshape(blocks, block_len, head_local, head_dim)
    grad_raw = inv_rms * (grad_norm - normed * jnp.mean(grad_norm * normed, axis=-1, keepdims=True))
    grad_bf = grad_raw.astype(jnp.bfloat16)
    grad_scores = jnp.einsum(
        "bthe,bshe->bhts", grad_bf, value_rows, preferred_element_type=jnp.float32
    )
    grad_scores = jnp.where(mask_tri, grad_scores, 0.0).astype(jnp.bfloat16)
    block_qg = jnp.einsum("bthd,bthe->bhde", queries, grad_bf, preferred_element_type=jnp.float32)
    own_grad = jnp.sum(block_qg, axis=0)
    later_state = prefix(own_grad, "ctx", add_states, zero_state, True)
    reversed_sum = jnp.cumsum(block_qg[::-1], axis=0)[::-1]
    local_after = jnp.concatenate([reversed_sum[1:], jnp.zeros_like(block_qg[:1])], axis=0)
    after = later_state[None] + local_after
    grad_q = jnp.einsum(
        "bthe,bhde->bthd", grad_bf.astype(jnp.float32), states, precision=highest
    ) + jnp.einsum("bhts,bshd->bthd", grad_scores, key_rows, preferred_element_type=jnp.float32)
    grad_k = jnp.einsum(
        "bshe,bhde->bshd", value_rows.astype(jnp.float32), after, precision=highest
    ) + jnp.einsum("bhts,bthd->bshd", grad_scores, queries, preferred_element_type=jnp.float32)
    grad_v = jnp.einsum(
        "bshd,bhde->bshe", key_rows.astype(jnp.float32), after, precision=highest
    ) + jnp.einsum("bhts,bthe->bshe", scores_bf, grad_bf, preferred_element_type=jnp.float32)
    grad_proj = (
        jnp.stack([grad_q, grad_k, grad_v], axis=3)
        .astype(jnp.bfloat16)
        .reshape(tok_rows, head_local * 3 * head_dim)
    )
    vocab_proj = contract_rows(one_hot.astype(jnp.bfloat16), grad_proj)
    vocab_cot = contract_rows(one_hot.astype(jnp.bfloat16), out_grad)
    summed_vocab, summed_wout, summed_gain, grad_init, summed_cot = lax.psum(
        (vocab_proj, grad_wout_local, grad_gain_local, own_grad, vocab_cot), "ctx"
    )
    summed_wqkv = lax.dot_general(
        embed_table.astype(jnp.float32),
        summed_vocab,
        (((0,), (0,)), ((), ())),
        precision=highest,
        preferred_element_type=jnp.float32,
    )
    head_table = lax.dot_general(
        summed_vocab,
        w_qkv.astype(jnp.float32),
        (((1,), (1,)), ((), ())),
        precision=highest,
        preferred_element_type=jnp.float32,
    )
    grad_table = lax.psum(head_table, "head") + summed_cot
    ctx_pos = lax.axis_index("ctx")
    width_rows = summed_wqkv.shape[0] // lax.axis_size("ctx")
    own_wqkv = lax.dynamic_slice_in_dim(summed_wqkv, ctx_pos * width_rows, width_rows, 0)
    own_wout = lax.dynamic_slice_in_dim(summed_wout, ctx_pos * width_rows, width_rows, 1)
    return (layer_out, own_wqkv, own_wout, summed_gain, grad_init, grad_table)


def solution(mesh):
    in_specs = (
        P(("parts", "ctx")),
        P(),
        P(None, "head"),
        P("head"),
        P("head", None),
        P("head", None, None),
        P(("parts", "ctx"), None),
    )
    out_specs = (
        P(("parts", "ctx"), "head"),
        P(("parts", "ctx"), "head"),
        P(("parts", "head"), "ctx"),
        P(("parts", "head")),
        P(("parts", "head"), None, None),
        P("parts", None),
    )
    return jax.shard_map(
        per_device, mesh=mesh, in_specs=in_specs, out_specs=out_specs, check_vma=False
    )
```

profile of v0, /device:TPU:0, one launch (start us, length us, event | category | flops | bytes accessed | tf_op | source)
XLA Modules:
  0.0 317.2 jit_solution(2077347792032638478)
XLA Ops:
  8.8 2.7 fusion.13
  13.6 3.0 convolution_convert_fusion.1
  16.5 2.6 copy.49
  19.1 1.8 copy.89
  24.0 2.3 fusion.48
  26.3 18.0 %all-gather = f32[8,128,128]{2,1,0:T(8,128)} all-gather(f32[2,128,128]{2,1,0:T(8,128)S(1)} %get-tuple-element.134), channel_id=2, replica_groups=mesh['parts'=2,'ctx'=4,'head'=4] {'ctx'}, dimensions={0}, use_global_device_ids=true | all-gather | bytes 655360 | tf_op jit(solution)/shard_map/all_gather | solution.py:16
  49.2 2.1 broadcast_multiply_fusion
  51.3 2.7 reshape.58
  54.0 2.2 copy.59
  56.3 1.8 multiply_reduce_fusion
  64.3 2.4 rev.4
  69.0 2.2 slice.23
  71.2 19.9 %all-gather.1 = f32[8,128,128]{2,1,0:T(8,128)} all-gather(f32[2,128,128]{2,1,0:T(8,128)S(1)} %get-tuple-element.138), channel_id=3, replica_groups=mesh['parts'=2,'ctx'=4,'head'=4] {'ctx'}, dimensions={0}, use_global_device_ids=true | all-gather | bytes 655360 | tf_op jit(solution)/shard_map/all_gather | solution.py:16
  91.2 3.1 while.23
  94.3 2.5 fusion.18
  104.6 116.2 %all-reduce.8.cloned.1.call-done = (f32[256,768]{1,0:T(8,128)}, f32[256,1024]{1,0:T(8,128)}, f32[2,128,128]{2,1,0:T(8,128)}, f32[256,1024]{1,0:T(8,128)}) async-done(((f32[256,768]{1,0:T(8,128)}, f32[256,1024]{1,0:T(8,128)}, f32[2,128,128]{2,1,0:T(8,128)}, f32[256,1024]{1,0:T(8,128)}), (f32[256,768]{1,0:T(8,128)}, f32[256,1024]{1,0:T(8,128)}, f32[2,128,128]{2,1,0:T(8,128)}, ...) | async-done | bytes 3014672 | tf_op jit(solution)/shard_map/psum | solution.py:122
  220.8 4.2 %fusion.53 = f32[256,1024]{1,0:T(8,128)} fusion(f32[256,768]{1,0:T(8,128)} %get-tuple-element.121, bf16[1024,768]{1,0:T(8,128)(2,1)} %param.13), kind=kOutput, calls=%fused_computation.80 | convolution fusion | flops 2415919104 | bytes 3407872 | tf_op jit(solution)/shard_map/dot_general | solution.py:132
  225.0 2.7 fusion.22
  230.3 1.8 fusion.12
  232.1 10.0 %psum.44 = f32[256]{0:T(256)} all-reduce(f32[256]{0:T(256)S(1)} %fusion.12), channel_id=1, replica_groups=mesh['parts'=2,'ctx'=4,'head'=4] {'ctx'}, use_global_device_ids=true, to_apply=%region_14.15 | all-reduce | flops 256 | bytes 2048 | tf_op jit(solution)/shard_map/psum | solution.py:122
  246.4 13.7 %all-reduce.6.cloned.1.call-done = f32[256,1024]{1,0:T(8,128)} async-done(((f32[256,1024]{1,0:T(8,128)}), f32[256,1024]{1,0:T(8,128)}) %all-reduce.6.cloned.1.call-update) | async-done | bytes 1048592 | tf_op jit(solution)/shard_map/psum | solution.py:139
  260.1 2.7 add.133
  262.8 44.9 %reduce-scatter.2.cloned.1.call-done = f32[1024,256]{1,0:T(8,128)} async-done(((f32[1024,1024]{1,0:T(8,128)}), f32[1024,256]{1,0:T(8,128)}) %reduce-scatter.2.cloned.1.call-update) | async-done | bytes 1048592 | tf_op jit(solution)/shard_map/reduce_scatter | solution.py:85
  307.7 2.3 add_convert_fusion
  (104 shorter events, 38.1 us)
Async XLA Ops:
  7.2 1.6 copy-start
  7.2 4.2 %copy-start.28 = (s32[1024]{0:T(1024)S(1)}, s32[1024]{0:T(1024)}, u32[]{:S(2)}) copy-start(s32[1024]{0:T(1024)} %param.11) | copy-start | bytes 12292
  7.2 4.2 %copy-start.18 = (bf16[256,1024]{1,0:T(8,128)(2,1)S(1)}, bf16[256,1024]{1,0:T(8,128)(2,1)}, u32[]{:S(2)}) copy-start(bf16[256,1024]{1,0:T(8,128)(2,1)} %param.12) | copy-start | bytes 1572868
  7.2 213.6 %all-reduce.8.cloned.1.call-start = ((), (), s32[]{:S(2)}) async-start(), calls=%async_computation.3 | async-start | bytes 6029312 | tf_op jit(solution)/shard_map/psum | solution.py:122
  11.4 2.1 copy-start.23
  22.4 24.2 %copy-start.4 = (bf16[8,128,2,1,128]{4,1,2,0,3:T(8,128)(2,1)}, bf16[8,128,2,1,128]{4,1,2,0,3:T(8,128)(2,1)S(1)}, u32[]{:S(2)}) copy-start(bf16[8,128,2,1,128]{4,1,2,0,3:T(8,128)(2,1)S(1)} %copy.88) | copy-start | bytes 1572868
  45.8 1.9 copy-start.10
  46.1 3.1 copy-start.20
  56.3 1.9 copy-start.3
  58.1 3.4 %copy-start.1 = (f32[8,128,2,128]{1,3,2,0:T(8,128)}, f32[8,128,2,128]{1,3,2,0:T(8,128)S(1)}, u32[]{:S(2)}) copy-start(f32[8,128,2,128]{1,3,2,0:T(8,128)S(1)} %get-tuple-element.126) | copy-start | bytes 3145732
  58.1 1.8 copy-start.11
  59.8 3.0 copy-start.5
  64.3 6.9 %copy-start.24 = (f32[2,128,128]{2,1,0:T(8,128)}, f32[2,128,128]{2,1,0:T(8,128)S(1)}, u32[]{:S(2)}) copy-start(f32[2,128,128]{2,1,0:T(8,128)S(1)} %get-tuple-element.138) | copy-start | bytes 393220
  94.2 2.6 copy-start.8
  94.2 2.6 copy-start.9
  94.2 3.6 %copy-start.22 = (bf16[8,128,2,128]{1,3,2,0:T(8,128)(2,1)S(1)}, bf16[8,128,2,128]{1,3,2,0:T(8,128)(2,1)}, u32[]{:S(2)}) copy-start(bf16[8,128,2,128]{1,3,2,0:T(8,128)(2,1)} %get-tuple-element.131) | copy-start | bytes 1572868
  98.2 1.7 copy-start.12
  98.2 1.7 copy-start.13
  104.5 155.6 %all-reduce.6.cloned.1.call-start = ((), (), s32[]{:S(2)}) async-start(), calls=%async_computation.2 | async-start | bytes 2097152 | tf_op jit(solution)/shard_map/psum | solution.py:139
  220.8 4.2 %copy-start.17 = (bf16[256,1024]{1,0:T(8,128)(2,1)S(1)}, bf16[256,1024]{1,0:T(8,128)(2,1)}, u32[]{:S(2)}) copy-start(bf16[256,1024]{1,0:T(8,128)(2,1)} %param.15) | copy-start | bytes 1572868
  225.0 82.8 %reduce-scatter.2.cloned.1.call-start = ((), (), s32[]{:S(2)}) async-start(), calls=%async_computation.1 | async-start | bytes 5242880 | tf_op jit(solution)/shard_map/reduce_scatter | solution.py:85
  230.2 11.8 %copy-start.15 = (f32[256,768]{1,0:T(8,128)S(1)}, f32[256,768]{1,0:T(8,128)}, u32[]{:S(2)}) copy-start(f32[256,768]{1,0:T(8,128)} %get-tuple-element.121) | copy-start | bytes 2359300
  230.3 11.8 %copy-start.19 = (bf16[256,1024]{1,0:T(8,128)(2,1)S(1)}, bf16[256,1024]{1,0:T(8,128)(2,1)}, u32[]{:S(2)}) copy-start(bf16[256,1024]{1,0:T(8,128)(2,1)} %param.12) | copy-start | bytes 1572868
  260.1 49.9 %copy-start.26 = (f32[2,128,128]{2,1,0:T(8,128)S(1)}, f32[2,128,128]{2,1,0:T(8,128)}, u32[]{:S(2)}) copy-start(f32[2,128,128]{2,1,0:T(8,128)} %get-tuple-element.241) | copy-start | bytes 393220
  (8 other events, 10.5 us)
Sparse Core Ops, SparseCore 0:
  104.6 116.0 all-reduce.7
  225.1 34.9 all-reduce.5
  262.8 44.8 reduce-scatter.1
where the time goes:
time: 318 us; the launch traced here: 317 us
  waiting for transfers between devices  175 us (55%)
  blocking collectives  47.9 us (15%)
  matrix products  34.4 us (11%)
  local copies, waits for them, and re-layouts  30.1 us (9%)
  other arithmetic  15.4 us (5%)
  between operations  14.2 us (4%)
    psum x1, waiting for transfers between devices, per_device(): lax.psum((vocab_proj, grad_wout_local, grad_gain_local, own_grad, vocab_c...  116 us
    reduce_scatter x1, waiting for transfers between devices, per_device(): lax.psum_scatter(head_terms, 'head', scatter_dimension=1, tiled=True)  44.9 us
    all_gather x2, blocking collectives, prefix(): gathered = lax.all_gather(part, axis)  37.9 us
    psum x1, waiting for transfers between devices, per_device(): grad_table = lax.psum(head_table, 'head') + summed_cot  13.7 us
    unnamed x63, local copies, waits for them, and re-layouts  11.4 us
    psum x1, blocking collectives, per_device(): lax.psum((vocab_proj, grad_wout_local, grad_gain_local, own_grad, vocab_c...  10 us
  transfers between devices with their start and end apart: 3, of which 3 were waited for; matrix products, arithmetic and copies ran while one was open for 4% of the time, Pallas kernels for 0%

commit v1 on v0

--- a/solution.py
+++ b/solution.py
@@ -1,6 +1,9 @@
+import functools
 import jax
 import jax.numpy as jnp
 from jax import lax
+from jax.experimental import pallas as pl
+from jax.experimental.pallas import tpu as pltpu
 from jax.sharding import PartitionSpec as P
 
 BLOCK = 128
@@ -144,6 +147,443 @@
     return (layer_out, own_wqkv, own_wout, summed_gain, grad_init, grad_table)
 
 
+F32 = jnp.float32
+BF16 = jnp.bfloat16
+CHUNKS = 4
+
+
+def nn(left, right):
+    return lax.dot_general(left, right, (((1,), (0,)), ((), ())), preferred_element_type=F32)
+
+
+def split(value):
+    high = value.astype(BF16)
+    return high, (value - high.astype(F32)).astype(BF16)
+
+
+def layer_kernel(
+    dims,
+    ids, table, wqkv, gain, wout, init, cot,
+    layer_out, grad_wqkv, grad_wout, grad_gain, grad_init, grad_table,
+    hot, tables, proj, gproj, scores, kv_loc, qg_loc, gattn, local_kv, grad_bf, attn_bf,
+    kv_own, kv_recv, kv_stage, qg_own, qg_recv, qg_stage,
+    wo_send, wo_recv, attn_send, attn_recv, gw_own, gw_recv,
+    voc_own, voc_recv, voc_stage, head_part, core_recv, pair_sum, cross_recv,
+    kv_ss, kv_rs, qg_ss, qg_rs, wo_ss, wo_rs, at_ss, at_rs, gw_ss, gw_rs,
+    voc_ss, voc_rs, tab_ss, tab_rs,
+):
+    C, tok, vocab, width, heads, dh = dims
+    blocks = tok // BLOCK
+    cols = heads * dh
+    three = 3 * cols
+    part = lax.axis_index("parts")
+    c = lax.axis_index("ctx")
+    h = lax.axis_index("head")
+    core = lax.rem(h, 2)
+    sib = h + 1 - 2 * core
+    across = lax.rem(h + 2, 4)
+    diag = lax.rem(sib + 2, 4)
+    peers = (sib, across, diag)
+    far_end = C - 1
+    near = c // (C // 2)
+    own_cols = pl.ds(pl.multiple_of(h * cols, cols), cols)
+
+    def remote(src, dst, ss, rs, ctx_to, head_to):
+        return pltpu.make_async_remote_copy(
+            src_ref=src, dst_ref=dst, send_sem=ss, recv_sem=rs,
+            device_id=(part, ctx_to, head_to), device_id_type=pl.DeviceIdType.MESH,
+        )
+
+    barrier = pltpu.get_barrier_semaphore()
+    for step in range(1, C):
+        pl.semaphore_signal(barrier, inc=1, device_id=(part, lax.rem(c + step, C), h),
+                            device_id_type=pl.DeviceIdType.MESH)
+    for peer in peers:
+        pl.semaphore_signal(barrier, inc=1, device_id=(part, c, peer),
+                            device_id_type=pl.DeviceIdType.MESH)
+
+    def has_recv(d):
+        return jnp.where(d == 0, c > 0, c < far_end)
+
+    def has_send(d):
+        return jnp.where(d == 0, c < far_end, c > 0)
+
+    def line_copy(d, i, recv, stage, ss, rs):
+        to = jnp.clip(c + 1 - 2 * d, 0, far_end)
+        return remote(stage.at[d, i], recv.at[d, i], ss.at[d, i], rs.at[d, i], to, h)
+
+    def line(d, i, own, recv, stage, ss, rs):
+        @pl.when(has_recv(d))
+        def _():
+            line_copy(d, i, recv, stage, ss, rs).wait_recv()
+
+        @pl.when(jnp.logical_not(has_recv(d)))
+        def _():
+            recv[d, i] = jnp.zeros(recv.shape[2:], F32)
+
+        @pl.when(has_send(d))
+        def _():
+            stage[d, i] = own[i] + recv[d, i]
+            line_copy(d, i, recv, stage, ss, rs).start()
+
+    def line_sent(d, i, recv, stage, ss, rs):
+        @pl.when(has_send(d))
+        def _():
+            line_copy(d, i, recv, stage, ss, rs).wait_send()
+
+    kv = (kv_own, kv_recv, kv_stage, kv_ss, kv_rs)
+    qg = (qg_own, qg_recv, qg_stage, qg_ss, qg_rs)
+    voc = (voc_own, voc_recv, voc_stage, voc_ss, voc_rs)
+
+    hot[...] = (lax.broadcasted_iota(jnp.int32, (vocab, tok), 0) == ids[...]).astype(BF16)
+    tables[:, :three] = nn(table[...], wqkv[...]).astype(BF16)
+    tables[:, three:] = table[:, own_cols]
+
+    def project(i, carry):
+        at = pl.ds(pl.multiple_of(i * 256, 256), 256)
+        proj[at, :] = contract_rows(hot[:, at], tables[...]).astype(BF16)
+        return carry
+
+    lax.fori_loop(0, tok // 256, project, 0)
+
+    kv_own[...] = jnp.zeros_like(kv_own)
+
+    def qkv(b, head):
+        at = pl.ds(pl.multiple_of(b * BLOCK, BLOCK), BLOCK)
+        base = head * 3 * dh
+        return (proj[at, base:base + dh], proj[at, base + dh:base + 2 * dh],
+                proj[at, base + 2 * dh:base + 3 * dh])
+
+    def key_values(b, carry):
+        for head in range(heads):
+            _, k, v = qkv(b, head)
+            kv_loc[b, head] = kv_own[head]
+            kv_own[head] = kv_own[head] + contract_rows(k, v)
+        return carry
+
+    lax.fori_loop(0, blocks, key_values, 0)
+
+    pl.semaphore_wait(barrier, C - 1 + len(peers))
+
+    def kv_step(place):
+        @pl.when(c == place)
+        def _():
+            for head in range(heads):
+                line(0, head, *kv)
+
+    kv_step(0)
+
+    def wo_copy(n):
+        return remote(wo_send.at[peers[n]], wo_recv.at[h], wo_ss.at[n], wo_rs.at[n], c, peers[n])
+
+    for block in range(4):
+        wo_send[block] = wout[:, block * cols:(block + 1) * cols].astype(F32)
+    for n in range(3):
+        wo_copy(n).start()
+
+    def cotangent(i, carry):
+        at = pl.ds(pl.multiple_of(i * 256, 256), 256)
+        gattn[at, :] = contract_cols(cot[at, :], wout[...])
+        return carry
+
+    lax.fori_loop(0, tok // 256, cotangent, 0)
+    kv_step(1)
+
+    mask = lower_mask(BLOCK)
+
+    def score(b, carry):
+        for head in range(heads):
+            q, k, _ = qkv(b, head)
+            scores[b, head] = jnp.where(mask, contract_cols(q, k), 0.0).astype(BF16)
+        return carry
+
+    lax.fori_loop(0, blocks, score, 0)
+    kv_step(2)
+
+    per = vocab // CHUNKS
+    for i in range(CHUNKS):
+        voc_own[i, :, three:] = nn(hot[i * per:(i + 1) * per, :], cot[:, own_cols])
+    for place in range(3, C):
+        kv_step(place)
+
+    qg_own[...] = jnp.zeros_like(qg_own)
+    for head in range(heads):
+        kv_own[head] = init[head] + kv_recv[0, head]
+
+    def forward(b, carry):
+        at = pl.ds(pl.multiple_of(b * BLOCK, BLOCK), BLOCK)
+        for head in range(heads):
+            q, k, v = qkv(b, head)
+            mine = slice(head * dh, (head + 1) * dh)
+            state = kv_loc[b, head] + kv_own[head]
+            kv_loc[b, head] = state
+            high, low = split(state)
+            raw = nn(q, high) + nn(q, low) + nn(scores[b, head], v)
+            inv = lax.rsqrt(jnp.mean(raw * raw, axis=-1, keepdims=True) + EPS)
+            normed = raw * inv
+            g_row = gain[head:head + 1, :]
+            attn = (normed * g_row).astype(BF16)
+            attn_bf[at, mine] = attn
+            attn_send[at, mine] = attn.astype(F32)
+            ga = gattn[at, mine]
+            qg_own[heads, head:head + 1, :] += jnp.sum(ga * normed, axis=0, keepdims=True)
+            dn = ga * g_row
+            g = inv * (dn - normed * jnp.mean(dn * normed, axis=-1, keepdims=True))
+            g = g.astype(BF16)
+            grad_bf[at, mine] = g
+            outer = contract_rows(q, g)
+            qg_loc[b, head] = outer
+            qg_own[head] += outer
+        return carry
+
+    lax.fori_loop(0, blocks, forward, 0)
+
+    at_sib = remote(attn_send, attn_recv.at[h], at_ss.at[0], at_rs.at[0], c, sib)
+    at_across = remote(attn_send, attn_recv.at[h], at_ss.at[1], at_rs.at[1], c, across)
+    at_relay = remote(attn_recv.at[across], attn_recv.at[across], at_ss.at[2], at_rs.at[2], c, sib)
+
+    at_end = jnp.logical_or(c == 0, c == far_end)
+
+    def qg_step(where, d):
+        @pl.when(where)
+        def _():
+            for piece in range(heads + 1):
+                line(d, piece, *qg)
+
+    qg_step(at_end, near)
+    at_sib.start()
+    at_across.start()
+
+    def weight(i, carry):
+        gw_own[i] = contract_rows(
+            attn_bf[...], cot[:, pl.ds(pl.multiple_of(i * cols, cols), cols)])
+        return carry
+
+    lax.fori_loop(0, C, weight, 0)
+    qg_step(jnp.logical_not(at_end), near)
+
+    def backward(b, carry):
+        at = pl.ds(pl.multiple_of(b * BLOCK, BLOCK), BLOCK)
+        for head in range(heads):
+            q, k, v = qkv(b, head)
+            base = head * 3 * dh
+            g = grad_bf[at, head * dh:(head + 1) * dh]
+            high, low = split(kv_loc[b, head])
+            gs = jnp.where(mask, contract_cols(g, v), 0.0).astype(BF16)
+            dq = contract_cols(g, high) + contract_cols(g, low) + nn(gs, k)
+            gproj[at, base:base + dh] = dq.astype(BF16)
+            local_kv[at, head * 2 * dh:head * 2 * dh + dh] = contract_rows(gs, q)
+            local_kv[at, head * 2 * dh + dh:(head + 1) * 2 * dh] = contract_rows(scores[b, head], g)
+        return carry
+
+    half = blocks // 2
+    lax.fori_loop(0, half, backward, 0)
+    qg_step(jnp.logical_not(at_end), 1 - near)
+    lax.fori_loop(half, blocks, backward, 0)
+    qg_step(at_end, 1 - near)
+
+    def gw_copy(step):
+        to = lax.rem(c + step, C)
+        return remote(gw_own.at[to], gw_recv.at[step - 1], gw_ss.at[step - 1],
+                      gw_rs.at[step - 1], to, h)
+
+    for step in range(1, C):
+        gw_copy(step).start()
+
+    for head in range(heads):
+        grad_init[head] = qg_own[head] + (qg_recv[0, head] + qg_recv[1, head])
+    grad_gain[...] = (qg_own[heads] + (qg_recv[0, heads] + qg_recv[1, heads]))[:heads, :]
+    for head in range(heads):
+        kv_own[head] = qg_recv[1, head]
+
+    def later(step, carry):
+        b = blocks - 1 - step
+        at = pl.ds(pl.multiple_of(b * BLOCK, BLOCK), BLOCK)
+        for head in range(heads):
+            _, k, v = qkv(b, head)
+            base = head * 3 * dh
+            after = kv_own[head]
+            high, low = split(after)
+            kv_own[head] = after + qg_loc[b, head]
+            dk = local_kv[at, head * 2 * dh:head * 2 * dh + dh]
+            dv = local_kv[at, head * 2 * dh + dh:(head + 1) * 2 * dh]
+            dk = dk + contract_cols(v, high) + contract_cols(v, low)
+            dv = dv + nn(k, high) + nn(k, low)
+            gproj[at, base + dh:base + 2 * dh] = dk.astype(BF16)
+            gproj[at, base + 2 * dh:base + 3 * dh] = dv.astype(BF16)
+        return carry
+
+    lax.fori_loop(0, blocks, later, 0)
+
+    for i in range(CHUNKS):
+        voc_own[i, :, :three] = nn(hot[i * per:(i + 1) * per, :], gproj[...])
+
+        @pl.when(at_end)
+        def _():
+            line(near, i, *voc)
+
+    at_across.wait_recv()
+    at_relay.start()
+
+    half_rows = per // 2
+    my_half = pl.ds(pl.multiple_of(core * half_rows, half_rows), half_rows)
+    sib_half = pl.ds(pl.multiple_of((1 - core) * half_rows, half_rows), half_rows)
+
+    def core_copy(i):
+        return remote(head_part.at[i, sib_half, :], core_recv.at[i],
+                      tab_ss.at[0, i], tab_rs.at[0, i], c, sib)
+
+    def cross_copy(i):
+        return remote(pair_sum.at[i], cross_recv.at[i], tab_ss.at[1, i], tab_rs.at[1, i], c, across)
+
+    def final_copy(i):
+        rows = pl.ds(pl.multiple_of(i * per + core * half_rows, half_rows), half_rows)
+        return remote(grad_table.at[rows, :], grad_table.at[rows, :],
+                      tab_ss.at[2, i], tab_rs.at[2, i], c, sib)
+
+    def start_head(i):
+        total = voc_own[i] + (voc_recv[0, i] + voc_recv[1, i])
+        voc_own[i] = total
+        high, low = split(total[:, :three])
+        head_part[i] = contract_cols(high, wqkv[...]) + contract_cols(low, wqkv[...])
+        head_part[i, :, own_cols] = head_part[i, :, own_cols] + total[:, three:]
+        core_copy(i).start()
+
+    def start_cross(i):
+        core_copy(i).wait_recv()
+        pair_sum[i] = head_part[i, my_half, :] + core_recv[i]
+        cross_copy(i).start()
+
+    def start_final(i):
+        cross_copy(i).wait_recv()
+        rows = pl.ds(pl.multiple_of(i * per + core * half_rows, half_rows), half_rows)
+        grad_table[rows, :] = pair_sum[i] + cross_recv[i]
+        final_copy(i).start()
+
+    for i in range(CHUNKS + 1):
+        if i < CHUNKS:
+            @pl.when(jnp.logical_not(at_end))
+            def _():
+                line(near, i, *voc)
+        if i > 0:
+            @pl.when(jnp.logical_not(at_end))
+            def _():
+                line(1 - near, i - 1, *voc)
+
+            @pl.when(at_end)
+            def _():
+                line(1 - near, i - 1, *voc)
+
+            start_head(i - 1)
+            if i > 1:
+                start_cross(i - 2)
+            if i > 2:
+                start_final(i - 3)
+
+    start_cross(CHUNKS - 1)
+
+    at_sib.wait_recv()
+    at_relay.wait_recv()
+    for n in range(3):
+        remote(wo_send.at[peers[n]], wo_recv.at[peers[n]], wo_ss.at[n], wo_rs.at[n], c, peers[n]).wait_recv()
+    wo_recv[h] = wout[:, own_cols].astype(F32)
+
+    def out_rows(i, carry):
+        at = pl.ds(pl.multiple_of(i * 256, 256), 256)
+        mixed = nn(attn_bf[at, :], wo_recv[h].astype(BF16))
+        for peer in peers:
+            mixed = mixed + nn(attn_recv[peer, at, :].astype(BF16), wo_recv[peer].astype(BF16))
+        layer_out[at, :] = (proj[at, three:].astype(F32) + mixed).astype(BF16)
+        return carry
+
+    lax.fori_loop(0, tok // 256, out_rows, 0)
+    start_final(CHUNKS - 2)
+
+    rows = pl.ds(pl.multiple_of(c * (width // C), width // C), width // C)
+    total_w = jnp.zeros((width // C, three), F32)
+    for i in range(CHUNKS):
+        high, low = split(voc_own[i, :, :three])
+        mine = table[i * per:(i + 1) * per, rows]
+        total_w = total_w + contract_rows(mine, high) + contract_rows(mine, low)
+    grad_wqkv[...] = total_w
+    start_final(CHUNKS - 1)
+
+    for step in range(1, C):
+        gw_copy(step).wait_recv()
+    grad_wout[...] = (gw_own[c] + gw_recv[0]) + (gw_recv[1] + gw_recv[2])
+
+    for i in range(CHUNKS):
+        other = pl.ds(pl.multiple_of(i * per + (1 - core) * half_rows, half_rows), half_rows)
+        remote(grad_table.at[other, :], grad_table.at[other, :],
+               tab_ss.at[2, i], tab_rs.at[2, i], c, sib).wait_recv()
+        core_copy(i).wait_send()
+        cross_copy(i).wait_send()
+        final_copy(i).wait_send()
+        for d in range(2):
+            line_sent(d, i, *voc[1:])
+    for head in range(heads):
+        line_sent(0, head, *kv[1:])
+    for piece in range(heads + 1):
+        for d in range(2):
+            line_sent(d, piece, *qg[1:])
+    for n in range(3):
+        wo_copy(n).wait_send()
+    for step in range(1, C):
+        gw_copy(step).wait_send()
+    at_sib.wait_send()
+    at_across.wait_send()
+    at_relay.wait_send()
+
+
+def one_kernel(event_ids, embed_table, w_qkv, norm_gain, w_out, init_state, out_grad):
+    tok, = event_ids.shape
+    vocab, width = embed_table.shape
+    heads, dh, _ = init_state.shape
+    C = lax.axis_size("ctx")
+    cols = heads * dh
+    three = 3 * cols
+    blocks = tok // BLOCK
+    per = vocab // CHUNKS
+    vmem = lambda *shape: pltpu.VMEM(shape, F32)
+    half = lambda *shape: pltpu.VMEM(shape, BF16)
+    dma = lambda *shape: pltpu.SemaphoreType.DMA(shape)
+    shapes = [
+        half(vocab, tok), half(vocab, three + cols), half(tok, three + cols), half(tok, three),
+        half(blocks, heads, BLOCK, BLOCK), vmem(blocks, heads, dh, dh), vmem(blocks, heads, dh, dh),
+        vmem(tok, cols), vmem(tok, 2 * cols), half(tok, cols), half(tok, cols),
+        vmem(heads, dh, dh), vmem(1, heads, dh, dh), vmem(1, heads, dh, dh),
+        vmem(heads + 1, dh, dh), vmem(2, heads + 1, dh, dh), vmem(2, heads + 1, dh, dh),
+        vmem(4, cols, cols), vmem(4, cols, cols), vmem(tok, cols), vmem(4, tok, cols),
+        vmem(C, cols, width // C), vmem(C - 1, cols, width // C),
+        vmem(CHUNKS, per, width), vmem(2, CHUNKS, per, width), vmem(2, CHUNKS, per, width),
+        vmem(CHUNKS, per, width), vmem(CHUNKS, per // 2, width), vmem(CHUNKS, per // 2, width),
+        vmem(CHUNKS, per // 2, width),
+        dma(1, heads), dma(1, heads), dma(2, heads + 1), dma(2, heads + 1), dma(3), dma(3),
+        dma(3), dma(3), dma(C - 1), dma(C - 1), dma(2, CHUNKS), dma(2, CHUNKS),
+        dma(3, CHUNKS), dma(3, CHUNKS),
+    ]
+    outs = pl.pallas_call(
+        functools.partial(layer_kernel, (C, tok, vocab, width, heads, dh)),
+        out_shape=(
+            jax.ShapeDtypeStruct((tok, cols), BF16),
+            jax.ShapeDtypeStruct((width // C, three), F32),
+            jax.ShapeDtypeStruct((cols, width // C), F32),
+            jax.ShapeDtypeStruct((heads, dh), F32),
+            jax.ShapeDtypeStruct((heads, dh, dh), F32),
+            jax.ShapeDtypeStruct((vocab, width), F32),
+        ),
+        in_specs=[pl.BlockSpec(memory_space=pltpu.VMEM)] * 7,
+        out_specs=(pl.BlockSpec(memory_space=pltpu.VMEM),) * 6,
+        scratch_shapes=shapes,
+        compiler_params=pltpu.CompilerParams(
+            collective_id=0, has_side_effects=True, vmem_limit_bytes=56 * 1024 * 1024
+        ),
+    )(event_ids.reshape(1, tok), embed_table, w_qkv, norm_gain.reshape(heads, dh), w_out,
+      init_state, out_grad)
+    layer_out, grad_wqkv, grad_wout, grad_gain, grad_init, grad_table = outs
+    return layer_out, grad_wqkv, grad_wout, grad_gain.reshape(cols), grad_init, grad_table
+
+
 def solution(mesh):
     in_specs = (
         P(("parts", "ctx")),
@@ -162,6 +602,7 @@
         P(("parts", "head"), None, None),
         P("parts", None),
     )
+    fits = mesh.shape["ctx"] == 4 and mesh.shape["head"] == 4
     return jax.shard_map(
-        per_device, mesh=mesh, in_specs=in_specs, out_specs=out_specs, check_vma=False
-    )
+        one_kernel if fits else per_device, mesh=mesh, in_specs=in_specs, out_specs=out_specs, check_vma=False
+    )

time: 318 us -> 111 us (0.35)
  waiting for transfers between devices: 175 us -> 0 us
  Pallas kernels: 0 us -> 103 us
  blocking collectives: 47.9 us -> 0 us
  matrix products: 34.4 us -> 0 us
  local copies, waits for them, and re-layouts: 30.1 us -> 6.94 us
  other arithmetic: 15.4 us -> 0 us
  between operations: 14.2 us -> 0.68 us
    psum x2 -> x0, waiting for transfers between devices: 130 us -> none  [the longest x1 116 us: per_device(): lax.psum((vocab_proj, grad_wout_local, grad_gain_local, own_grad, vocab_c...]
    pallas_call x0 -> x1, Pallas kernels: none -> 103 us  [one_kernel(): pl.pallas_call(functools.partial(layer_kernel, (C, tok, vocab, width, hea...]
    reduce_scatter x1 -> x0, waiting for transfers between devices: 44.9 us -> none  [per_device(): lax.psum_scatter(head_terms, 'head', scatter_dimension=1, tiled=True)]
    all_gather x2 -> x0, blocking collectives: 37.9 us -> none  [prefix(): gathered = lax.all_gather(part, axis)]
    dot_general x21 -> x0, matrix products: 34.4 us -> none  [the longest x3 6.04 us: contract_rows(): lax.dot_general(left, right, (((0,), (0,)), ((), ())), preferred_element_...]
    psum x1 -> x0, blocking collectives: 10 us -> none  [per_device(): lax.psum((vocab_proj, grad_wout_local, grad_gain_local, own_grad, vocab_c...]
    reshape x3 -> x0, local copies, waits for them, and re-layouts: 6.26 us -> none  [the longest x2 4.97 us: per_device(): (grad_attn * norm_gain).reshape(blocks, block_len, head_local, head_dim)]
    add x5 -> x0, other arithmetic: 5.55 us -> none  [the longest x3 2.81 us: add_states(): return earlier + later_one]
  transfers between devices with their start and end apart: 3 -> 0, of which waited for: 3 -> 0; matrix products, arithmetic and copies ran while one was open for 4% -> 0% of each run, Pallas kernels for 0% -> 0%
where the time goes in v1:
time: 111 us
  Pallas kernels  103 us (93%)
  local copies, waits for them, and re-layouts  6.94 us (6%)
    pallas_call x1, Pallas kernels, one_kernel(): pl.pallas_call(functools.partial(layer_kernel, (C, tok, vocab, width, hea...  103 us
    unnamed x14, local copies, waits for them, and re-layouts  6.94 us

profile of v1, /device:TPU:0, one launch (start us, length us, event | category | flops | bytes accessed | tf_op | source)
XLA Modules:
  0.0 110.6 jit_solution(4314444639834238228)
XLA Ops:
  0.6 103.0 %shard_map.118 = (bf16[1024,256]{1,0:T(8,128)(2,1)}, f32[256,768]{1,0:T(8,128)}, f32[256,256]{1,0:T(8,128)}, f32[2,128]{1,0:T(2,128)}, f32[2,128,128]{2,1,0:T(8,128)}, /*index=5*/f32[256,1024]{1,0:T(8,128)}) custom-call(s32[1,1024]{1,0:T(1,128)} %bitcast.3, bf16[256,1024]{1,0:T(8,128)(2,1)} %table.1, bf16[1024,768]{1,0:T(8,128)(2,1)} %wqkv.1, ...), custom_call_target="tpu_custom_call" | custom-call | tf_op jit(solution)/shard_map/pallas_call | solution.py:565
  103.6 0.0 copy-start.1
  103.6 0.0 copy-start.3
  103.6 0.0 copy-start.2
  103.6 0.0 copy-start
  103.6 2.0 %copy.19 = bf16[1024,256]{1,0:T(8,128)(2,1)} copy(bf16[1024,256]{1,0:T(8,128)(2,1)} %get-tuple-element.24) | data formatting | bytes 1048576
  105.6 2.1 %copy.20 = f32[256,768]{1,0:T(8,128)} copy(f32[256,768]{1,0:T(8,128)} %get-tuple-element.25) | data formatting | bytes 1572864
  107.7 0.0 copy-done.1
  107.7 0.7 copy.21
  108.4 0.0 copy-done.3
  108.4 0.6 copy.22
  108.9 0.0 copy-done.2
  108.9 0.7 copy.23
  109.6 0.0 copy-done
  109.6 1.0 copy.24
Async XLA Ops:
  103.6 4.1 %copy-start.1 = (f32[256,256]{1,0:T(8,128)S(1)}, f32[256,256]{1,0:T(8,128)}, u32[]{:S(2)}) copy-start(f32[256,256]{1,0:T(8,128)} %get-tuple-element.26) | copy-start | bytes 786436
  103.6 4.8 %copy-start.3 = (f32[2,128]{1,0:T(2,128)S(1)}, f32[2,128]{1,0:T(2,128)}, u32[]{:S(2)}) copy-start(f32[2,128]{1,0:T(2,128)} %get-tuple-element.15) | copy-start | bytes 3076
  103.6 5.3 %copy-start.2 = (f32[2,128,128]{2,1,0:T(8,128)S(1)}, f32[2,128,128]{2,1,0:T(8,128)}, u32[]{:S(2)}) copy-start(f32[2,128,128]{2,1,0:T(8,128)} %get-tuple-element.28) | copy-start | bytes 393220
  103.6 6.0 %copy-start = (f32[256,1024]{1,0:T(8,128)S(1)}, f32[256,1024]{1,0:T(8,128)}, u32[]{:S(2)}) copy-start(f32[256,1024]{1,0:T(8,128)} %get-tuple-element.29) | copy-start | bytes 3145732

commit v2 on v1

--- a/solution.py
+++ b/solution.py
@@ -149,7 +149,7 @@
 
 F32 = jnp.float32
 BF16 = jnp.bfloat16
-CHUNKS = 4
+CHUNKS = 8
 
 
 def nn(left, right):
@@ -166,10 +166,10 @@
     ids, table, wqkv, gain, wout, init, cot,
     layer_out, grad_wqkv, grad_wout, grad_gain, grad_init, grad_table,
     hot, tables, proj, gproj, scores, kv_loc, qg_loc, gattn, local_kv, grad_bf, attn_bf,
-    kv_own, kv_recv, kv_stage, qg_own, qg_recv, qg_stage,
+    kv_own, kv_recv, kv_stage, qg_own, qg_recv, qg_stage, gn_own, gn_recv, gn_stage, ct_own, ct_recv, ct_stage,
     wo_send, wo_recv, attn_send, attn_recv, gw_own, gw_recv,
     voc_own, voc_recv, voc_stage, head_part, core_recv, pair_sum, cross_recv,
-    kv_ss, kv_rs, qg_ss, qg_rs, wo_ss, wo_rs, at_ss, at_rs, gw_ss, gw_rs,
+    kv_ss, kv_rs, qg_ss, qg_rs, gn_ss, gn_rs, ct_ss, ct_rs, wo_ss, wo_rs, at_ss, at_rs, gw_ss, gw_rs,
     voc_ss, voc_rs, tab_ss, tab_rs,
 ):
     C, tok, vocab, width, heads, dh = dims
@@ -233,9 +233,24 @@
 
     kv = (kv_own, kv_recv, kv_stage, kv_ss, kv_rs)
     qg = (qg_own, qg_recv, qg_stage, qg_ss, qg_rs)
+    gn = (gn_own, gn_recv, gn_stage, gn_ss, gn_rs)
+    ct = (ct_own, ct_recv, ct_stage, ct_ss, ct_rs)
     voc = (voc_own, voc_recv, voc_stage, voc_ss, voc_rs)
 
     hot[...] = (lax.broadcasted_iota(jnp.int32, (vocab, tok), 0) == ids[...]).astype(BF16)
+    quarter = vocab // 4
+    for i in range(4):
+        ct_own[i] = nn(hot[i * quarter:(i + 1) * quarter, :], cot[:, own_cols])
+    at_end = jnp.logical_or(c == 0, c == far_end)
+
+    def ct_step(where, d):
+        @pl.when(where)
+        def _():
+            for piece in range(4):
+                line(d, piece, *ct)
+
+    pl.semaphore_wait(barrier, C - 1 + len(peers))
+    ct_step(at_end, near)
     tables[:, :three] = nn(table[...], wqkv[...]).astype(BF16)
     tables[:, three:] = table[:, own_cols]
 
@@ -263,7 +278,6 @@
 
     lax.fori_loop(0, blocks, key_values, 0)
 
-    pl.semaphore_wait(barrier, C - 1 + len(peers))
 
     def kv_step(place):
         @pl.when(c == place)
@@ -301,12 +315,12 @@
     kv_step(2)
 
     per = vocab // CHUNKS
-    for i in range(CHUNKS):
-        voc_own[i, :, three:] = nn(hot[i * per:(i + 1) * per, :], cot[:, own_cols])
     for place in range(3, C):
         kv_step(place)
+    ct_step(jnp.logical_not(at_end), near)
 
     qg_own[...] = jnp.zeros_like(qg_own)
+    gn_own[...] = jnp.zeros_like(gn_own)
     for head in range(heads):
         kv_own[head] = init[head] + kv_recv[0, head]
 
@@ -326,7 +340,7 @@
             attn_bf[at, mine] = attn
             attn_send[at, mine] = attn.astype(F32)
             ga = gattn[at, mine]
-            qg_own[heads, head:head + 1, :] += jnp.sum(ga * normed, axis=0, keepdims=True)
+            gn_own[0, head:head + 1, :] += jnp.sum(ga * normed, axis=0, keepdims=True)
             dn = ga * g_row
             g = inv * (dn - normed * jnp.mean(dn * normed, axis=-1, keepdims=True))
             g = g.astype(BF16)
@@ -336,19 +350,21 @@
             qg_own[head] += outer
         return carry
 
-    lax.fori_loop(0, blocks, forward, 0)
+    half = blocks // 2
+    lax.fori_loop(0, half, forward, 0)
+    ct_step(jnp.logical_not(at_end), 1 - near)
+    lax.fori_loop(half, blocks, forward, 0)
 
     at_sib = remote(attn_send, attn_recv.at[h], at_ss.at[0], at_rs.at[0], c, sib)
     at_across = remote(attn_send, attn_recv.at[h], at_ss.at[1], at_rs.at[1], c, across)
     at_relay = remote(attn_recv.at[across], attn_recv.at[across], at_ss.at[2], at_rs.at[2], c, sib)
 
-    at_end = jnp.logical_or(c == 0, c == far_end)
-
     def qg_step(where, d):
         @pl.when(where)
         def _():
-            for piece in range(heads + 1):
+            for piece in range(heads):
                 line(d, piece, *qg)
+            line(d, 0, *gn)
 
     qg_step(at_end, near)
     at_sib.start()
@@ -360,6 +376,20 @@
         return carry
 
     lax.fori_loop(0, C, weight, 0)
+
+    near_place = jnp.where(near == 0, c, far_end - c)
+
+    def gw_to(k):
+        place = k + jnp.where(k >= near_place, 1, 0)
+        return jnp.where(near == 0, place, far_end - place)
+
+    def gw_copy(to):
+        return remote(gw_own.at[to], gw_recv.at[c], gw_ss.at[to], gw_rs.at[c], to, h)
+
+    def gw_start(k):
+        gw_copy(gw_to(k)).start()
+
+    gw_start(0)
     qg_step(jnp.logical_not(at_end), near)
 
     def backward(b, carry):
@@ -376,23 +406,16 @@
             local_kv[at, head * 2 * dh + dh:(head + 1) * 2 * dh] = contract_rows(scores[b, head], g)
         return carry
 
-    half = blocks // 2
     lax.fori_loop(0, half, backward, 0)
     qg_step(jnp.logical_not(at_end), 1 - near)
     lax.fori_loop(half, blocks, backward, 0)
     qg_step(at_end, 1 - near)
 
-    def gw_copy(step):
-        to = lax.rem(c + step, C)
-        return remote(gw_own.at[to], gw_recv.at[step - 1], gw_ss.at[step - 1],
-                      gw_rs.at[step - 1], to, h)
-
-    for step in range(1, C):
-        gw_copy(step).start()
+    gw_start(1)
 
     for head in range(heads):
         grad_init[head] = qg_own[head] + (qg_recv[0, head] + qg_recv[1, head])
-    grad_gain[...] = (qg_own[heads] + (qg_recv[0, heads] + qg_recv[1, heads]))[:heads, :]
+    grad_gain[...] = (gn_own[0] + (gn_recv[0, 0] + gn_recv[1, 0]))[:heads, :]
     for head in range(heads):
         kv_own[head] = qg_recv[1, head]
 
@@ -416,14 +439,13 @@
     lax.fori_loop(0, blocks, later, 0)
 
     for i in range(CHUNKS):
-        voc_own[i, :, :three] = nn(hot[i * per:(i + 1) * per, :], gproj[...])
+        voc_own[i] = nn(hot[i * per:(i + 1) * per, :], gproj[...])
 
         @pl.when(at_end)
         def _():
             line(near, i, *voc)
 
-    at_across.wait_recv()
-    at_relay.start()
+    ct_step(at_end, 1 - near)
 
     half_rows = per // 2
     my_half = pl.ds(pl.multiple_of(core * half_rows, half_rows), half_rows)
@@ -444,9 +466,12 @@
     def start_head(i):
         total = voc_own[i] + (voc_recv[0, i] + voc_recv[1, i])
         voc_own[i] = total
-        high, low = split(total[:, :three])
-        head_part[i] = contract_cols(high, wqkv[...]) + contract_cols(low, wqkv[...])
-        head_part[i, :, own_cols] = head_part[i, :, own_cols] + total[:, three:]
+        both = contract_cols(jnp.concatenate(split(total), axis=0), wqkv[...])
+        head_part[i] = both[:per] + both[per:]
+        piece, off = i * per // quarter, i * per % quarter
+        rows = slice(off, off + per)
+        cot_sum = ct_own[piece, rows, :] + (ct_recv[0, piece, rows, :] + ct_recv[1, piece, rows, :])
+        head_part[i, :, own_cols] = head_part[i, :, own_cols] + cot_sum
         core_copy(i).start()
 
     def start_cross(i):
@@ -460,57 +485,55 @@
         grad_table[rows, :] = pair_sum[i] + cross_recv[i]
         final_copy(i).start()
 
+    def out_rows(i):
+        at = slice(i * (tok // 4), (i + 1) * (tok // 4))
+        mixed = nn(attn_bf[at, :], wo_recv[h].astype(BF16))
+        for peer in peers:
+            mixed = mixed + nn(attn_recv[peer, at, :].astype(BF16), wo_recv[peer].astype(BF16))
+        layer_out[at, :] = (proj[at, three:].astype(F32) + mixed).astype(BF16)
+
+    wo_recv[h] = wout[:, own_cols].astype(F32)
+
     for i in range(CHUNKS + 1):
         if i < CHUNKS:
             @pl.when(jnp.logical_not(at_end))
             def _():
                 line(near, i, *voc)
+        if i == 2:
+            at_across.wait_recv()
+            at_relay.start()
         if i > 0:
-            @pl.when(jnp.logical_not(at_end))
-            def _():
-                line(1 - near, i - 1, *voc)
-
-            @pl.when(at_end)
-            def _():
-                line(1 - near, i - 1, *voc)
-
+            line(1 - near, i - 1, *voc)
             start_head(i - 1)
             if i > 1:
                 start_cross(i - 2)
             if i > 2:
                 start_final(i - 3)
-
+        if i == 3:
+            at_sib.wait_recv()
+            at_relay.wait_recv()
+            for n in range(3):
+                remote(wo_send.at[peers[n]], wo_recv.at[peers[n]], wo_ss.at[n], wo_rs.at[n],
+                       c, peers[n]).wait_recv()
+        if 3 <= i < 7:
+            out_rows(i - 3)
+
+    gw_start(2)
     start_cross(CHUNKS - 1)
-
-    at_sib.wait_recv()
-    at_relay.wait_recv()
-    for n in range(3):
-        remote(wo_send.at[peers[n]], wo_recv.at[peers[n]], wo_ss.at[n], wo_rs.at[n], c, peers[n]).wait_recv()
-    wo_recv[h] = wout[:, own_cols].astype(F32)
-
-    def out_rows(i, carry):
-        at = pl.ds(pl.multiple_of(i * 256, 256), 256)
-        mixed = nn(attn_bf[at, :], wo_recv[h].astype(BF16))
-        for peer in peers:
-            mixed = mixed + nn(attn_recv[peer, at, :].astype(BF16), wo_recv[peer].astype(BF16))
-        layer_out[at, :] = (proj[at, three:].astype(F32) + mixed).astype(BF16)
-        return carry
-
-    lax.fori_loop(0, tok // 256, out_rows, 0)
     start_final(CHUNKS - 2)
 
     rows = pl.ds(pl.multiple_of(c * (width // C), width // C), width // C)
-    total_w = jnp.zeros((width // C, three), F32)
-    for i in range(CHUNKS):
-        high, low = split(voc_own[i, :, :three])
-        mine = table[i * per:(i + 1) * per, rows]
-        total_w = total_w + contract_rows(mine, high) + contract_rows(mine, low)
-    grad_wqkv[...] = total_w
+    total_w = voc_own[...].reshape(vocab, three)
+    high, low = split(total_w)
+    grad_wqkv[...] = contract_rows(table[:, rows], high) + contract_rows(table[:, rows], low)
     start_final(CHUNKS - 1)
 
+    gw_recv[c] = gw_own[c]
     for step in range(1, C):
-        gw_copy(step).wait_recv()
-    grad_wout[...] = (gw_own[c] + gw_recv[0]) + (gw_recv[1] + gw_recv[2])
+        source = lax.rem(c + step, C)
+        remote(gw_own.at[source], gw_recv.at[source], gw_ss.at[source], gw_rs.at[source],
+               source, h).wait_recv()
+    grad_wout[...] = (gw_recv[0] + gw_recv[1]) + (gw_recv[2] + gw_recv[3])
 
     for i in range(CHUNKS):
         other = pl.ds(pl.multiple_of(i * per + (1 - core) * half_rows, half_rows), half_rows)
@@ -523,16 +546,28 @@
             line_sent(d, i, *voc[1:])
     for head in range(heads):
         line_sent(0, head, *kv[1:])
-    for piece in range(heads + 1):
-        for d in range(2):
+    for d in range(2):
+        for piece in range(heads):
             line_sent(d, piece, *qg[1:])
+        line_sent(d, 0, *gn[1:])
+        for piece in range(4):
+            line_sent(d, piece, *ct[1:])
     for n in range(3):
         wo_copy(n).wait_send()
-    for step in range(1, C):
-        gw_copy(step).wait_send()
+    for k in range(C - 1):
+        gw_copy(gw_to(k)).wait_send()
     at_sib.wait_send()
     at_across.wait_send()
     at_relay.wait_send()
+
+
+def hand_over(*refs):
+    sems = refs[12]
+    copies = [pltpu.make_async_copy(refs[i], refs[i + 6], sems.at[i]) for i in range(6)]
+    for copy in copies:
+        copy.start()
+    for copy in copies:
+        copy.wait()
 
 
 def one_kernel(event_ids, embed_table, w_qkv, norm_gain, w_out, init_state, out_grad):
@@ -552,14 +587,17 @@
         half(blocks, heads, BLOCK, BLOCK), vmem(blocks, heads, dh, dh), vmem(blocks, heads, dh, dh),
         vmem(tok, cols), vmem(tok, 2 * cols), half(tok, cols), half(tok, cols),
         vmem(heads, dh, dh), vmem(1, heads, dh, dh), vmem(1, heads, dh, dh),
-        vmem(heads + 1, dh, dh), vmem(2, heads + 1, dh, dh), vmem(2, heads + 1, dh, dh),
+        vmem(heads, dh, dh), vmem(2, heads, dh, dh), vmem(2, heads, dh, dh),
+        vmem(1, 8, dh), vmem(2, 1, 8, dh), vmem(2, 1, 8, dh),
+        vmem(4, vocab // 4, cols), vmem(2, 4, vocab // 4, cols), vmem(2, 4, vocab // 4, cols),
         vmem(4, cols, cols), vmem(4, cols, cols), vmem(tok, cols), vmem(4, tok, cols),
-        vmem(C, cols, width // C), vmem(C - 1, cols, width // C),
-        vmem(CHUNKS, per, width), vmem(2, CHUNKS, per, width), vmem(2, CHUNKS, per, width),
+        vmem(C, cols, width // C), vmem(C, cols, width // C),
+        vmem(CHUNKS, per, three), vmem(2, CHUNKS, per, three), vmem(2, CHUNKS, per, three),
         vmem(CHUNKS, per, width), vmem(CHUNKS, per // 2, width), vmem(CHUNKS, per // 2, width),
         vmem(CHUNKS, per // 2, width),
-        dma(1, heads), dma(1, heads), dma(2, heads + 1), dma(2, heads + 1), dma(3), dma(3),
-        dma(3), dma(3), dma(C - 1), dma(C - 1), dma(2, CHUNKS), dma(2, CHUNKS),
+        dma(1, heads), dma(1, heads), dma(2, heads), dma(2, heads),
+        dma(2, 1), dma(2, 1), dma(2, 4), dma(2, 4), dma(3), dma(3),
+        dma(3), dma(3), dma(C), dma(C), dma(2, CHUNKS), dma(2, CHUNKS),
         dma(3, CHUNKS), dma(3, CHUNKS),
     ]
     outs = pl.pallas_call(
@@ -580,6 +618,13 @@
         ),
     )(event_ids.reshape(1, tok), embed_table, w_qkv, norm_gain.reshape(heads, dh), w_out,
       init_state, out_grad)
+    outs = pl.pallas_call(
+        hand_over,
+        out_shape=tuple(jax.ShapeDtypeStruct(out.shape, out.dtype) for out in outs),
+        in_specs=[pl.BlockSpec(memory_space=pl.ANY)] * 6,
+        out_specs=(pl.BlockSpec(memory_space=pl.ANY),) * 6,
+        scratch_shapes=[pltpu.SemaphoreType.DMA((6,))],
+    )(*outs)
     layer_out, grad_wqkv, grad_wout, grad_gain, grad_init, grad_table = outs
     return layer_out, grad_wqkv, grad_wout, grad_gain.reshape(cols), grad_init, grad_table
 

time: 111 us -> 186 us (1.68)
  Pallas kernels: 103 us -> 185 us
  local copies, waits for them, and re-layouts: 6.94 us -> 0 us
    pallas_call x0 -> x1, Pallas kernels: none -> 84.6 us  [one_kernel(): pl.pallas_call(hand_over, out_shape=tuple((jax.ShapeDtypeStruct(out.shape...]
    unnamed x14 -> x0, local copies, waits for them, and re-layouts: 6.94 us -> none
    pallas_call x1, Pallas kernels: 103 us -> 101 us  [one_kernel(): pl.pallas_call(functools.partial(layer_kernel, (C, tok, vocab, width, hea...]
where the time goes in v2:
time: 186 us
  Pallas kernels  185 us (99%)
    pallas_call x1, Pallas kernels, one_kernel(): pl.pallas_call(functools.partial(layer_kernel, (C, tok, vocab, width, hea...  101 us
    pallas_call x1, Pallas kernels, one_kernel(): pl.pallas_call(hand_over, out_shape=tuple((jax.ShapeDtypeStruct(out.shape...  84.6 us

profile of v2, /device:TPU:0, one launch (start us, length us, event | category | flops | bytes accessed | tf_op | source)
XLA Modules:
  0.0 185.8 jit_solution(16810383385177392653)
XLA Ops:
  0.6 100.6 %shard_map.118 = (bf16[1024,256]{1,0:T(8,128)(2,1)}, f32[256,768]{1,0:T(8,128)}, f32[256,256]{1,0:T(8,128)}, f32[2,128]{1,0:T(2,128)}, f32[2,128,128]{2,1,0:T(8,128)}, /*index=5*/f32[256,1024]{1,0:T(8,128)}) custom-call(s32[1,1024]{1,0:T(1,128)} %bitcast.3, bf16[256,1024]{1,0:T(8,128)(2,1)} %table.1, bf16[1024,768]{1,0:T(8,128)(2,1)} %wqkv.1, ...), custom_call_target="tpu_custom_call" | custom-call | tf_op jit(solution)/shard_map/pallas_call | solution.py:603
  101.3 84.6 %shard_map.119 = (bf16[1024,256]{1,0:T(8,128)(2,1)}, f32[256,768]{1,0:T(8,128)}, f32[256,256]{1,0:T(8,128)}, f32[2,128]{1,0:T(2,128)}, f32[2,128,128]{2,1,0:T(8,128)}, /*index=5*/f32[256,1024]{1,0:T(8,128)}) custom-call(bf16[1024,256]{1,0:T(8,128)(2,1)} %get-tuple-element.18.refs_0_, f32[256,768]{1,0:T(8,128)} %get-tuple-element.19.refs_1_, ...), custom_call_target="tpu_custom_call" | custom-call | tf_op jit(solution)/shard_map/pallas_call | solution.py:621

commit v3 on v2

--- a/solution.py
+++ b/solution.py
@@ -150,6 +150,7 @@
 F32 = jnp.float32
 BF16 = jnp.bfloat16
 CHUNKS = 8
+GW_AT = 5
 
 
 def nn(left, right):
@@ -167,7 +168,7 @@
     layer_out, grad_wqkv, grad_wout, grad_gain, grad_init, grad_table,
     hot, tables, proj, gproj, scores, kv_loc, qg_loc, gattn, local_kv, grad_bf, attn_bf,
     kv_own, kv_recv, kv_stage, qg_own, qg_recv, qg_stage, gn_own, gn_recv, gn_stage, ct_own, ct_recv, ct_stage,
-    wo_send, wo_recv, attn_send, attn_recv, gw_own, gw_recv,
+    wo_send, wo_recv, attn_send, attn_recv, gw_own, gw_recv, gw_stage,
     voc_own, voc_recv, voc_stage, head_part, core_recv, pair_sum, cross_recv,
     kv_ss, kv_rs, qg_ss, qg_rs, gn_ss, gn_rs, ct_ss, ct_rs, wo_ss, wo_rs, at_ss, at_rs, gw_ss, gw_rs,
     voc_ss, voc_rs, tab_ss, tab_rs,
@@ -377,19 +378,26 @@
 
     lax.fori_loop(0, C, weight, 0)
 
-    near_place = jnp.where(near == 0, c, far_end - c)
-
-    def gw_to(k):
-        place = k + jnp.where(k >= near_place, 1, 0)
+    def gw_block(place):
         return jnp.where(near == 0, place, far_end - place)
 
-    def gw_copy(to):
-        return remote(gw_own.at[to], gw_recv.at[c], gw_ss.at[to], gw_rs.at[c], to, h)
-
-    def gw_start(k):
-        gw_copy(gw_to(k)).start()
-
-    gw_start(0)
+    def gw_copy(d, place, source):
+        block = gw_block(place)
+        to = jnp.clip(c + 1 - 2 * d, 0, far_end)
+        return remote(source.at[d, block] if source is gw_stage else source.at[block],
+                      gw_recv.at[d, block], gw_ss.at[d, block], gw_rs.at[d, block], to, h)
+
+    def gw_pass(d, place):
+        block = gw_block(place)
+        gw_copy(d, place, gw_stage).wait_recv()
+        gw_stage[d, block] = gw_own[block] + gw_recv[d, block]
+        gw_copy(d, place, gw_stage).start()
+
+    @pl.when(at_end)
+    def _():
+        for place in range(C - 1, 1, -1):
+            gw_copy(near, place, gw_own).start()
+
     qg_step(jnp.logical_not(at_end), near)
 
     def backward(b, carry):
@@ -410,8 +418,6 @@
     qg_step(jnp.logical_not(at_end), 1 - near)
     lax.fori_loop(half, blocks, backward, 0)
     qg_step(at_end, 1 - near)
-
-    gw_start(1)
 
     for head in range(heads):
         grad_init[head] = qg_own[head] + (qg_recv[0, head] + qg_recv[1, head])
@@ -494,6 +500,11 @@
 
     wo_recv[h] = wout[:, own_cols].astype(F32)
 
+    @pl.when(jnp.logical_not(at_end))
+    def _():
+        for place in range(C - 1, 1, -1):
+            gw_pass(near, place)
+
     for i in range(CHUNKS + 1):
         if i < CHUNKS:
             @pl.when(jnp.logical_not(at_end))
@@ -509,6 +520,15 @@
                 start_cross(i - 2)
             if i > 2:
                 start_final(i - 3)
+        if i == GW_AT:
+            @pl.when(at_end)
+            def _():
+                gw_copy(near, 1, gw_own).start()
+
+            @pl.when(jnp.logical_not(at_end))
+            def _():
+                gw_pass(1 - near, 0)
+
         if i == 3:
             at_sib.wait_recv()
             at_relay.wait_recv()
@@ -518,7 +538,6 @@
         if 3 <= i < 7:
             out_rows(i - 3)
 
-    gw_start(2)
     start_cross(CHUNKS - 1)
     start_final(CHUNKS - 2)
 
@@ -528,12 +547,12 @@
     grad_wqkv[...] = contract_rows(table[:, rows], high) + contract_rows(table[:, rows], low)
     start_final(CHUNKS - 1)
 
-    gw_recv[c] = gw_own[c]
-    for step in range(1, C):
-        source = lax.rem(c + step, C)
-        remote(gw_own.at[source], gw_recv.at[source], gw_ss.at[source], gw_rs.at[source],
-               source, h).wait_recv()
-    grad_wout[...] = (gw_recv[0] + gw_recv[1]) + (gw_recv[2] + gw_recv[3])
+    grad_wout[...] = gw_own[c]
+    for d in range(2):
+        @pl.when(has_recv(d))
+        def _():
+            remote(gw_stage.at[d, c], gw_recv.at[d, c], gw_ss.at[d, c], gw_rs.at[d, c], c, h).wait_recv()
+            grad_wout[...] += gw_recv[d, c]
 
     for i in range(CHUNKS):
         other = pl.ds(pl.multiple_of(i * per + (1 - core) * half_rows, half_rows), half_rows)
@@ -554,20 +573,26 @@
             line_sent(d, piece, *ct[1:])
     for n in range(3):
         wo_copy(n).wait_send()
-    for k in range(C - 1):
-        gw_copy(gw_to(k)).wait_send()
+
+    @pl.when(at_end)
+    def _():
+        for place in range(1, C):
+            gw_copy(near, place, gw_own).wait_send()
+
+    @pl.when(jnp.logical_not(at_end))
+    def _():
+        for place in range(2, C):
+            gw_copy(near, place, gw_stage).wait_send()
+        gw_copy(1 - near, 0, gw_stage).wait_send()
+
     at_sib.wait_send()
     at_across.wait_send()
     at_relay.wait_send()
 
 
 def hand_over(*refs):
-    sems = refs[12]
-    copies = [pltpu.make_async_copy(refs[i], refs[i + 6], sems.at[i]) for i in range(6)]
-    for copy in copies:
-        copy.start()
-    for copy in copies:
-        copy.wait()
+    for i in range(6):
+        refs[i + 6][...] = refs[i][...]
 
 
 def one_kernel(event_ids, embed_table, w_qkv, norm_gain, w_out, init_state, out_grad):
@@ -591,13 +616,13 @@
         vmem(1, 8, dh), vmem(2, 1, 8, dh), vmem(2, 1, 8, dh),
         vmem(4, vocab // 4, cols), vmem(2, 4, vocab // 4, cols), vmem(2, 4, vocab // 4, cols),
         vmem(4, cols, cols), vmem(4, cols, cols), vmem(tok, cols), vmem(4, tok, cols),
-        vmem(C, cols, width // C), vmem(C, cols, width // C),
+        vmem(C, cols, width // C), vmem(2, C, cols, width // C), vmem(2, C, cols, width // C),
         vmem(CHUNKS, per, three), vmem(2, CHUNKS, per, three), vmem(2, CHUNKS, per, three),
         vmem(CHUNKS, per, width), vmem(CHUNKS, per // 2, width), vmem(CHUNKS, per // 2, width),
         vmem(CHUNKS, per // 2, width),
         dma(1, heads), dma(1, heads), dma(2, heads), dma(2, heads),
         dma(2, 1), dma(2, 1), dma(2, 4), dma(2, 4), dma(3), dma(3),
-        dma(3), dma(3), dma(C), dma(C), dma(2, CHUNKS), dma(2, CHUNKS),
+        dma(3), dma(3), dma(2, C), dma(2, C), dma(2, CHUNKS), dma(2, CHUNKS),
         dma(3, CHUNKS), dma(3, CHUNKS),
     ]
     outs = pl.pallas_call(
@@ -621,9 +646,8 @@
     outs = pl.pallas_call(
         hand_over,
         out_shape=tuple(jax.ShapeDtypeStruct(out.shape, out.dtype) for out in outs),
-        in_specs=[pl.BlockSpec(memory_space=pl.ANY)] * 6,
-        out_specs=(pl.BlockSpec(memory_space=pl.ANY),) * 6,
-        scratch_shapes=[pltpu.SemaphoreType.DMA((6,))],
+        in_specs=[pl.BlockSpec(memory_space=pltpu.VMEM)] * 6,
+        out_specs=(pl.BlockSpec(memory_space=pltpu.VMEM),) * 6,
     )(*outs)
     layer_out, grad_wqkv, grad_wout, grad_gain, grad_init, grad_table = outs
     return layer_out, grad_wqkv, grad_wout, grad_gain.reshape(cols), grad_init, grad_table

time: 186 us -> 100 us (0.54)
  Pallas kernels: 185 us -> 99.2 us
    pallas_call x1, Pallas kernels: 84.6 us -> 3.34 us  [one_kernel(): pl.pallas_call(hand_over, out_shape=tuple((jax.ShapeDtypeStruct(out.shape...]
    pallas_call x1, Pallas kernels: 101 us -> 95.8 us  [one_kernel(): pl.pallas_call(functools.partial(layer_kernel, (C, tok, vocab, width, hea...]
where the time goes in v3:
time: 100 us; the launch traced here: 99.8 us
  Pallas kernels  99.2 us (99%)
    pallas_call x1, Pallas kernels, one_kernel(): pl.pallas_call(functools.partial(layer_kernel, (C, tok, vocab, width, hea...  95.8 us
    pallas_call x1, Pallas kernels, one_kernel(): pl.pallas_call(hand_over, out_shape=tuple((jax.ShapeDtypeStruct(out.shape...  3.34 us

profile of v3, /device:TPU:0, one launch (start us, length us, event | category | flops | bytes accessed | tf_op | source)
XLA Modules:
  0.0 99.8 jit_solution(1460224989959299311)
XLA Ops:
  0.6 95.8 %shard_map.118 = (bf16[1024,256]{1,0:T(8,128)(2,1)}, f32[256,768]{1,0:T(8,128)}, f32[256,256]{1,0:T(8,128)}, f32[2,128]{1,0:T(2,128)}, f32[2,128,128]{2,1,0:T(8,128)}, /*index=5*/f32[256,1024]{1,0:T(8,128)}) custom-call(s32[1,1024]{1,0:T(1,128)} %bitcast.3, bf16[256,1024]{1,0:T(8,128)(2,1)} %table.1, bf16[1024,768]{1,0:T(8,128)(2,1)} %wqkv.1, ...), custom_call_target="tpu_custom_call" | custom-call | tf_op jit(solution)/shard_map/pallas_call | solution.py:628
  96.5 3.3 %shard_map.119 = (bf16[1024,256]{1,0:T(8,128)(2,1)}, f32[256,768]{1,0:T(8,128)}, f32[256,256]{1,0:T(8,128)}, f32[2,128]{1,0:T(2,128)}, f32[2,128,128]{2,1,0:T(8,128)}, /*index=5*/f32[256,1024]{1,0:T(8,128)}) custom-call(bf16[1024,256]{1,0:T(8,128)(2,1)} %get-tuple-element.18.refs_0_, f32[256,768]{1,0:T(8,128)} %get-tuple-element.19.refs_1_, ...), custom_call_target="tpu_custom_call" | custom-call | tf_op jit(solution)/shard_map/pallas_call | solution.py:646
